TPU v7x, 32 devices: a whole 2x2x4 slice. The times are simulated.
32 devices in a mesh: row: 8 (over z, y), col: 4 (over x, core).
Axes of the slice: x: 2, y: 2, z: 4, core: 2. Of those that a mesh axis runs over, the one named last changes fastest.
Arguments:
- vectors: float32 [4096, 512], P('row', 'col'), may hold values from -6 to 6
- reflectors: float32 [8, 1024, 512], P('row', 'col'), may hold values from -2 to 2
- factors: float32 [8, 512, 512], P('row', 'col'), may hold values from -2 to 2
Outputs:
- transformed: float32 [4096, 512], P('row', 'col')
All inputs are finite; a program needn't handle non-finite values.
Results may differ from a plain program's by a relative error of at most 0.0003.
Values sent between devices are 32-bit elements; how exact they have to be, the bound alone decides.
A program may use at most 64 MiB of HBM per device.

v0:
```python
import jax
import jax.numpy as jnp
from jax import lax
from jax.sharding import PartitionSpec as P


def passed_along(value, axis, steps):
    count = lax.axis_size(axis)
    first, last = (max(0, -steps), min(count, count - steps))
    return lax.ppermute(value, axis, [(source, source + steps) for source in range(first, last)])


def product(left, right):
    return jnp.dot(left, right, precision=lax.Precision.HIGHEST, preferred_element_type=jnp.float32)


def local(vectors, reflectors, factors):
    gathered, triangles = (
        lax.all_gather(reflectors, "col", axis=1, tiled=True),
        lax.all_gather(factors, "col", axis=1, tiled=True),
    )
    shaped = gathered[0]
    triangle = triangles[0]
    band_rows = triangle.shape[0]
    upper_part = shaped[:band_rows]
    lower_part = shaped[band_rows:]
    own_edge = vectors - product(upper_part, product(triangle, product(upper_part.T, vectors)))
    coupling = -product(product(upper_part, triangle), lower_part.T)

    def advance(turn, state):
        edge_rows = state[0]
        received = passed_along(edge_rows, "row", -1)
        return (own_edge + product(coupling, received), received)

    state = lax.fori_loop(0, lax.axis_size("row"), advance, (own_edge, jnp.zeros_like(own_edge)))
    below = state[1]
    stacked = jnp.concatenate([vectors, below], axis=0)
    updated = stacked - product(shaped, product(triangle, product(shaped.T, stacked)))
    returned = passed_along(updated[band_rows:], "row", 1)
    return jnp.where(lax.axis_index("row") == 0, updated[:band_rows], returned)


def solution(mesh):
    in_specs = (P("row", "col"), P("row", "col", None), P("row", "col", None))
    out_specs = P("row", "col")
    return jax.shard_map(local, mesh=mesh, in_specs=in_specs, out_specs=out_specs, check_vma=False)
```

profile of v0, /device:TPU:6, one launch (start us, length us, event | category | flops | bytes accessed | tf_op | source)
XLA Modules:
  0.0 183.9 jit_solution(4762481309715003011)
XLA Ops:
  9.1 22.7 %all-gather.3.cloned.1.call-done = f32[1,1024,512]{2,1,0:T(8,128)} async-done(((f32[1,256,512]{2,1,0:T(8,128)}), f32[1,1024,512]{2,1,0:T(8,128)}) %all-gather.3.cloned.1.call-update) | async-done | bytes 2097168 | tf_op jit(solution)/shard_map/all_gather | solution.py:19
  31.8 3.9 %fusion.17 = f32[512,128]{1,0:T(8,128)} fusion(f32[512,128]{1,0:T(8,128)} %param.5, f32[1,1024,512]{2,1,0:T(8,128)} %all-gather.3.cloned.1.call-done), kind=kOutput, calls=%fused_computation.18 | convolution fusion | flops 402653184 | bytes 1572864 | tf_op jit(solution)/shard_map/dot_general | solution.py:14
  35.7 14.4 %all-gather.5.cloned.1.call-done = f32[1,512,512]{2,1,0:T(8,128)} async-done(((f32[1,128,512]{2,1,0:T(8,128)}), f32[1,512,512]{2,1,0:T(8,128)}) %all-gather.5.cloned.1.call-update) | async-done | bytes 1048592 | tf_op jit(solution)/shard_map/all_gather | solution.py:20
  50.1 2.6 %fusion.15 = f32[128,512]{1,0:T(8,128)S(1)} fusion(f32[512,128]{1,0:T(8,128)} %fusion.17, f32[1,512,512]{2,1,0:T(8,128)} %all-gather.5.cloned.1.call-done), kind=kOutput, calls=%fused_computation.16 | convolution fusion | flops 402653184 | bytes 1572864 | tf_op jit(solution)/shard_map/dot_general | solution.py:14
  60.2 100.7 %while.12 = (s32[]{:T(128)}, f32[512,128]{1,0:T(8,128)}, f32[512,128]{1,0:T(8,128)}, f32[512,512]{1,0:T(8,128)S(1)}, f32[512,128]{1,0:T(8,128)S(1)}, /*index=5*/s32[]{:T(128)}) while((s32[]{:T(128)}, f32[512,128]{1,0:T(8,128)}, f32[512,128]{1,0:T(8,128)}, f32[512,512]{1,0:T(8,128)S(1)}, f32[512,128]{1,0:T(8,128)S(1)}, ...), condition=%wide.region_1.0_spmd, body=%wide.region_0.0_spmd.sunk | while | flops 402718720 | bytes 2883693 | solution.py:35
  62.6 9.3 %collective-permute-done = f32[512,128]{1,0:T(8,128)} collective-permute-done((f32[512,128]{1,0:T(8,128)}, f32[512,128]{1,0:T(8,128)}, u32[]{:S(2)}, u32[]{:S(2)}) %collective-permute-start) | collective-permute-done | bytes 262176 | tf_op jit(solution)/shard_map/while/body/eval_jaxpr/ppermute | solution.py:10
  71.9 2.6 %convolution_add_fusion.2 = f32[512,128]{1,0:T(8,128)} fusion(f32[512,128]{1,0:T(8,128)S(1)} %get-tuple-element.92, f32[512,512]{1,0:T(8,128)S(1)} %get-tuple-element.91, f32[512,128]{1,0:T(8,128)} %collective-permute-done), kind=kOutput, calls=%fused_computation.clone.1 | convolution fusion | flops 402718720 | bytes 1835008 | tf_op jit(solution)/shard_map/while/body/eval_jaxpr/dot_general | solution.py:14
  76.5 8.8 %collective-permute-done = f32[512,128]{1,0:T(8,128)} collective-permute-done((f32[512,128]{1,0:T(8,128)}, f32[512,128]{1,0:T(8,128)}, u32[]{:S(2)}, u32[]{:S(2)}) %collective-permute-start) | collective-permute-done | bytes 262176 | tf_op jit(solution)/shard_map/while/body/eval_jaxpr/ppermute | solution.py:10
  85.3 2.6 %convolution_add_fusion.2 = f32[512,128]{1,0:T(8,128)} fusion(f32[512,128]{1,0:T(8,128)S(1)} %get-tuple-element.92, f32[512,512]{1,0:T(8,128)S(1)} %get-tuple-element.91, f32[512,128]{1,0:T(8,128)} %collective-permute-done), kind=kOutput, calls=%fused_computation.clone.1 | convolution fusion | flops 402718720 | bytes 1835008 | tf_op jit(solution)/shard_map/while/body/eval_jaxpr/dot_general | solution.py:14
  89.9 7.9 %collective-permute-done = f32[512,128]{1,0:T(8,128)} collective-permute-done((f32[512,128]{1,0:T(8,128)}, f32[512,128]{1,0:T(8,128)}, u32[]{:S(2)}, u32[]{:S(2)}) %collective-permute-start) | collective-permute-done | bytes 262176 | tf_op jit(solution)/shard_map/while/body/eval_jaxpr/ppermute | solution.py:10
  97.7 2.6 %convolution_add_fusion.2 = f32[512,128]{1,0:T(8,128)} fusion(f32[512,128]{1,0:T(8,128)S(1)} %get-tuple-element.92, f32[512,512]{1,0:T(8,128)S(1)} %get-tuple-element.91, f32[512,128]{1,0:T(8,128)} %collective-permute-done), kind=kOutput, calls=%fused_computation.clone.1 | convolution fusion | flops 402718720 | bytes 1835008 | tf_op jit(solution)/shard_map/while/body/eval_jaxpr/dot_general | solution.py:14
  102.3 7.6 %collective-permute-done = f32[512,128]{1,0:T(8,128)} collective-permute-done((f32[512,128]{1,0:T(8,128)}, f32[512,128]{1,0:T(8,128)}, u32[]{:S(2)}, u32[]{:S(2)}) %collective-permute-start) | collective-permute-done | bytes 262176 | tf_op jit(solution)/shard_map/while/body/eval_jaxpr/ppermute | solution.py:10
  109.9 2.6 %convolution_add_fusion.2 = f32[512,128]{1,0:T(8,128)} fusion(f32[512,128]{1,0:T(8,128)S(1)} %get-tuple-element.92, f32[512,512]{1,0:T(8,128)S(1)} %get-tuple-element.91, f32[512,128]{1,0:T(8,128)} %collective-permute-done), kind=kOutput, calls=%fused_computation.clone.1 | convolution fusion | flops 402718720 | bytes 1835008 | tf_op jit(solution)/shard_map/while/body/eval_jaxpr/dot_general | solution.py:14
  114.4 7.6 %collective-permute-done = f32[512,128]{1,0:T(8,128)} collective-permute-done((f32[512,128]{1,0:T(8,128)}, f32[512,128]{1,0:T(8,128)}, u32[]{:S(2)}, u32[]{:S(2)}) %collective-permute-start) | collective-permute-done | bytes 262176 | tf_op jit(solution)/shard_map/while/body/eval_jaxpr/ppermute | solution.py:10
  122.0 2.6 %convolution_add_fusion.2 = f32[512,128]{1,0:T(8,128)} fusion(f32[512,128]{1,0:T(8,128)S(1)} %get-tuple-element.92, f32[512,512]{1,0:T(8,128)S(1)} %get-tuple-element.91, f32[512,128]{1,0:T(8,128)} %collective-permute-done), kind=kOutput, calls=%fused_computation.clone.1 | convolution fusion | flops 402718720 | bytes 1835008 | tf_op jit(solution)/shard_map/while/body/eval_jaxpr/dot_general | solution.py:14
  126.5 7.6 %collective-permute-done = f32[512,128]{1,0:T(8,128)} collective-permute-done((f32[512,128]{1,0:T(8,128)}, f32[512,128]{1,0:T(8,128)}, u32[]{:S(2)}, u32[]{:S(2)}) %collective-permute-start) | collective-permute-done | bytes 262176 | tf_op jit(solution)/shard_map/while/body/eval_jaxpr/ppermute | solution.py:10
  134.1 2.6 %convolution_add_fusion.2 = f32[512,128]{1,0:T(8,128)} fusion(f32[512,128]{1,0:T(8,128)S(1)} %get-tuple-element.92, f32[512,512]{1,0:T(8,128)S(1)} %get-tuple-element.91, f32[512,128]{1,0:T(8,128)} %collective-permute-done), kind=kOutput, calls=%fused_computation.clone.1 | convolution fusion | flops 402718720 | bytes 1835008 | tf_op jit(solution)/shard_map/while/body/eval_jaxpr/dot_general | solution.py:14
  138.6 7.6 %collective-permute-done = f32[512,128]{1,0:T(8,128)} collective-permute-done((f32[512,128]{1,0:T(8,128)}, f32[512,128]{1,0:T(8,128)}, u32[]{:S(2)}, u32[]{:S(2)}) %collective-permute-start) | collective-permute-done | bytes 262176 | tf_op jit(solution)/shard_map/while/body/eval_jaxpr/ppermute | solution.py:10
  146.2 2.6 %convolution_add_fusion.2 = f32[512,128]{1,0:T(8,128)} fusion(f32[512,128]{1,0:T(8,128)S(1)} %get-tuple-element.92, f32[512,512]{1,0:T(8,128)S(1)} %get-tuple-element.91, f32[512,128]{1,0:T(8,128)} %collective-permute-done), kind=kOutput, calls=%fused_computation.clone.1 | convolution fusion | flops 402718720 | bytes 1835008 | tf_op jit(solution)/shard_map/while/body/eval_jaxpr/dot_general | solution.py:14
  150.7 7.6 %collective-permute-done = f32[512,128]{1,0:T(8,128)} collective-permute-done((f32[512,128]{1,0:T(8,128)}, f32[512,128]{1,0:T(8,128)}, u32[]{:S(2)}, u32[]{:S(2)}) %collective-permute-start) | collective-permute-done | bytes 262176 | tf_op jit(solution)/shard_map/while/body/eval_jaxpr/ppermute | solution.py:10
  158.3 2.6 %convolution_add_fusion.2 = f32[512,128]{1,0:T(8,128)} fusion(f32[512,128]{1,0:T(8,128)S(1)} %get-tuple-element.92, f32[512,512]{1,0:T(8,128)S(1)} %get-tuple-element.91, f32[512,128]{1,0:T(8,128)} %collective-permute-done), kind=kOutput, calls=%fused_computation.clone.1 | convolution fusion | flops 402718720 | bytes 1835008 | tf_op jit(solution)/shard_map/while/body/eval_jaxpr/dot_general | solution.py:14
  162.1 2.3 %fusion.2 = f32[128,512]{1,0:T(8,128)S(1)} fusion(f32[1,1024,512]{2,1,0:T(8,128)S(1)} %copy-done, f32[512,128]{0,1:T(8,128)S(1)} %copy.8, f32[512,128]{0,1:T(8,128)} %copy-done.3), kind=kOutput, calls=%fused_computation.3 | convolution fusion | flops 805437440 | bytes 2883584 | tf_op jit(solution)/shard_map/dot_general | solution.py:14
  165.6 2.3 %fusion.7 = f32[1024,128]{0,1:T(8,128)S(1)} fusion(f32[128,512]{1,0:T(8,128)S(1)} %fusion.11, f32[1,1024,512]{2,1,0:T(8,128)S(1)} %copy-done, f32[512,128]{0,1:T(8,128)S(1)} %copy.8, f32[512,128]{0,1:T(8,128)S(1)} %copy-done.4), kind=kOutput, calls=%fused_computation.7 | convolution fusion | flops 805568512 | bytes 3407872 | tf_op jit(solution)/shard_map/dot_general | solution.py:14
  169.9 6.3 %collective-permute-done.1 = f32[512,128]{0,1:T(8,128)S(1)} collective-permute-done((f32[512,128]{0,1:T(8,128)S(1)}, f32[512,128]{0,1:T(8,128)S(1)}, u32[]{:S(2)}, u32[]{:S(2)}) %collective-permute-start.1) | collective-permute-done | bytes 262176 | tf_op jit(solution)/shard_map/ppermute | solution.py:10
  (35 shorter events, 30.7 us)
Async XLA Ops:
  6.5 25.3 %all-gather.3.cloned.1.call-start = ((), (), s32[]{:S(2)}) async-start(), calls=%async_computation | async-start | bytes 2621440 | tf_op jit(solution)/shard_map/all_gather | solution.py:19
  7.3 42.9 %all-gather.5.cloned.1.call-start = ((), (), s32[]{:S(2)}) async-start(), calls=%async_computation.1 | async-start | bytes 1310720 | tf_op jit(solution)/shard_map/all_gather | solution.py:20
  9.1 43.7 %copy-start.3 = (f32[512,128]{0,1:T(8,128)}, f32[512,128]{0,1:T(8,128)S(1)}, u32[]{:S(2)}) copy-start(f32[512,128]{0,1:T(8,128)S(1)} %copy.7) | copy-start | bytes 786436
  31.8 21.0 %copy-start = (f32[1,1024,512]{2,1,0:T(8,128)S(1)}, f32[1,1024,512]{2,1,0:T(8,128)}, u32[]{:S(2)}) copy-start(f32[1,1024,512]{2,1,0:T(8,128)} %all-gather.3.cloned.1.call-done) | copy-start | bytes 6291460
  50.1 6.3 %copy-start.1 = (f32[1,512,512]{2,1,0:T(8,128)S(1)}, f32[1,512,512]{2,1,0:T(8,128)}, u32[]{:S(2)}) copy-start(f32[1,512,512]{2,1,0:T(8,128)} %all-gather.5.cloned.1.call-done) | copy-start | bytes 3145732
  60.4 11.6 %collective-permute-start = (f32[512,128]{1,0:T(8,128)}, f32[512,128]{1,0:T(8,128)}, u32[]{:S(2)}, u32[]{:S(2)}) collective-permute-start(f32[512,128]{1,0:T(8,128)} %get-tuple-element.83), channel_id=1, source_target_pairs={{4,0},{8,4},{12,8},{16,12},{20,16},{24,20},{28,24},{5,1},{9,5},{13... | collective-permute-start | bytes 786440 | tf_op jit(solution)/shard_map/while/body/eval_jaxpr/ppermute | solution.py:10
  74.6 10.7 %collective-permute-start = (f32[512,128]{1,0:T(8,128)}, f32[512,128]{1,0:T(8,128)}, u32[]{:S(2)}, u32[]{:S(2)}) collective-permute-start(f32[512,128]{1,0:T(8,128)} %get-tuple-element.83), channel_id=1, source_target_pairs={{4,0},{8,4},{12,8},{16,12},{20,16},{24,20},{28,24},{5,1},{9,5},{13... | collective-permute-start | bytes 786440 | tf_op jit(solution)/shard_map/while/body/eval_jaxpr/ppermute | solution.py:10
  87.9 9.8 %collective-permute-start = (f32[512,128]{1,0:T(8,128)}, f32[512,128]{1,0:T(8,128)}, u32[]{:S(2)}, u32[]{:S(2)}) collective-permute-start(f32[512,128]{1,0:T(8,128)} %get-tuple-element.83), channel_id=1, source_target_pairs={{4,0},{8,4},{12,8},{16,12},{20,16},{24,20},{28,24},{5,1},{9,5},{13... | collective-permute-start | bytes 786440 | tf_op jit(solution)/shard_map/while/body/eval_jaxpr/ppermute | solution.py:10
  100.4 9.5 %collective-permute-start = (f32[512,128]{1,0:T(8,128)}, f32[512,128]{1,0:T(8,128)}, u32[]{:S(2)}, u32[]{:S(2)}) collective-permute-start(f32[512,128]{1,0:T(8,128)} %get-tuple-element.83), channel_id=1, source_target_pairs={{4,0},{8,4},{12,8},{16,12},{20,16},{24,20},{28,24},{5,1},{9,5},{13... | collective-permute-start | bytes 786440 | tf_op jit(solution)/shard_map/while/body/eval_jaxpr/ppermute | solution.py:10
  112.5 9.5 %collective-permute-start = (f32[512,128]{1,0:T(8,128)}, f32[512,128]{1,0:T(8,128)}, u32[]{:S(2)}, u32[]{:S(2)}) collective-permute-start(f32[512,128]{1,0:T(8,128)} %get-tuple-element.83), channel_id=1, source_target_pairs={{4,0},{8,4},{12,8},{16,12},{20,16},{24,20},{28,24},{5,1},{9,5},{13... | collective-permute-start | bytes 786440 | tf_op jit(solution)/shard_map/while/body/eval_jaxpr/ppermute | solution.py:10
  124.6 9.5 %collective-permute-start = (f32[512,128]{1,0:T(8,128)}, f32[512,128]{1,0:T(8,128)}, u32[]{:S(2)}, u32[]{:S(2)}) collective-permute-start(f32[512,128]{1,0:T(8,128)} %get-tuple-element.83), channel_id=1, source_target_pairs={{4,0},{8,4},{12,8},{16,12},{20,16},{24,20},{28,24},{5,1},{9,5},{13... | collective-permute-start | bytes 786440 | tf_op jit(solution)/shard_map/while/body/eval_jaxpr/ppermute | solution.py:10
  136.7 9.5 %collective-permute-start = (f32[512,128]{1,0:T(8,128)}, f32[512,128]{1,0:T(8,128)}, u32[]{:S(2)}, u32[]{:S(2)}) collective-permute-start(f32[512,128]{1,0:T(8,128)} %get-tuple-element.83), channel_id=1, source_target_pairs={{4,0},{8,4},{12,8},{16,12},{20,16},{24,20},{28,24},{5,1},{9,5},{13... | collective-permute-start | bytes 786440 | tf_op jit(solution)/shard_map/while/body/eval_jaxpr/ppermute | solution.py:10
  148.8 9.5 %collective-permute-start = (f32[512,128]{1,0:T(8,128)}, f32[512,128]{1,0:T(8,128)}, u32[]{:S(2)}, u32[]{:S(2)}) collective-permute-start(f32[512,128]{1,0:T(8,128)} %get-tuple-element.83), channel_id=1, source_target_pairs={{4,0},{8,4},{12,8},{16,12},{20,16},{24,20},{28,24},{5,1},{9,5},{13... | collective-permute-start | bytes 786440 | tf_op jit(solution)/shard_map/while/body/eval_jaxpr/ppermute | solution.py:10
  160.9 3.5 %copy-start.2 = (f32[1,512,512]{2,1,0:T(8,128)S(1)}, f32[1,512,512]{2,1,0:T(8,128)}, u32[]{:S(2)}) copy-start(f32[1,512,512]{2,1,0:T(8,128)} %all-gather.5.cloned.1.call-done) | copy-start | bytes 3145732
  162.1 3.5 %copy-start.4 = (f32[512,128]{0,1:T(8,128)S(1)}, f32[512,128]{0,1:T(8,128)}, u32[]{:S(2)}) copy-start(f32[512,128]{0,1:T(8,128)} %copy-done.3) | copy-start | bytes 786436
  167.9 8.3 %collective-permute-start.1 = (f32[512,128]{0,1:T(8,128)S(1)}, f32[512,128]{0,1:T(8,128)S(1)}, u32[]{:S(2)}, u32[]{:S(2)}) collective-permute-start(f32[512,128]{0,1:T(8,128)S(1)} %slice.27), channel_id=1, source_target_pairs={{0,4},{4,8},{8,12},{12,16},{16,20},{20,24},{24,28},{1,5},{5,9},{9,... | collective-permute-start | bytes 786440 | tf_op jit(solution)/shard_map/ppermute | solution.py:10
Sparse Core Ops, SparseCore 0:
  8.9 22.8 all-gather.2
  33.4 16.7 all-gather.4
where the time goes:
time: 186 us; the launch traced here: 184 us
  waiting for transfers between devices  109 us (59%)
  matrix products  39 us (21%)
  starting transfers between devices  17.6 us (9%)
  between operations  13.6 us (7%)
  local copies, waits for them, and re-layouts  4.9 us (3%)
    ppermute x9, waiting for transfers between devices, passed_along(): lax.ppermute(value, axis, [(source, source + steps) for source in range(f...  70.1 us
    dot_general x16, matrix products, product(): jnp.dot(left, right, precision=lax.Precision.HIGHEST, preferred_element_t...  39 us
    all_gather x1, waiting for transfers between devices, local(): lax.all_gather(reflectors, 'col', axis=1, tiled=True)  22.7 us
    ppermute x9, starting transfers between devices, passed_along(): lax.ppermute(value, axis, [(source, source + steps) for source in range(f...  17.5 us
    all_gather x1, waiting for transfers between devices, local(): lax.all_gather(factors, 'col', axis=1, tiled=True)  14.4 us
  transfers between devices with their start and end apart: 11, of which 11 were waited for; matrix products, arithmetic and copies ran while one was open for 3% of the time, Pallas kernels for 0%

commit v1 on v0

v1 whole, which is shorter than its diff:
```python
import functools

import jax
import jax.numpy as jnp
from jax import lax
from jax.experimental import pallas as pl
from jax.experimental.pallas import tpu as pltpu
from jax.sharding import PartitionSpec as P

MESH = pl.DeviceIdType.MESH
CHUNKS = 4
F32, BF16 = jnp.float32, jnp.bfloat16


def halves(value):
    high = value.astype(BF16)
    return high, (value - high.astype(F32)).astype(BF16)


def as_left(value):
    high, low = halves(value)
    return jnp.concatenate([high, high, low], axis=1)


def as_right(value, axis):
    high, low = halves(value)
    return jnp.concatenate([high, low, high], axis=axis)


def nn(left, right):
    return lax.dot_general(left, right, (((1,), (0,)), ((), ())), preferred_element_type=F32)


def nt(left, right):
    return lax.dot_general(left, right, (((1,), (1,)), ((), ())), preferred_element_type=F32)


def kernel(rows, cols, x_ref, v_ref, f_ref, out_ref,
           vg, fg, f3, u3, g3, h3, ct3, dt3, at, et, xt, xu3, zin, zout, osend, ret,
           gs_send, gs_recv, fw_send, fw_recv, z_send, z_recv, o_send, o_recv):
    row, col = lax.axis_index("row"), lax.axis_index("col")
    chips = cols // 2
    core, chip = lax.rem(col, 2), col // 2
    partner = chip * 2 + (1 - core)
    band = f3.shape[1]
    vrows, frows = v_ref.shape[1], f_ref.shape[1]
    half = vrows // 2
    width = xt.shape[0]
    part = width // CHUNKS
    first, last = row == 0, row == rows - 1

    barrier = pltpu.get_barrier_semaphore()

    def greet(device):
        pl.semaphore_signal(barrier, inc=1, device_id=device, device_id_type=MESH)

    greet({"col": partner})
    for d in range(1, chips):
        greet({"col": lax.rem(chip + d, chips) * 2 + core})

    @pl.when(row > 0)
    def _():
        greet({"row": row - 1})

    @pl.when(row < rows - 1)
    def _():
        greet({"row": row + 1})

    edges = jnp.where(first, 0, 1) + jnp.where(last, 0, 1)
    pl.semaphore_wait(barrier, chips + edges)

    def held(piece, owner):
        if piece == 0:
            return fg.at[pl.ds(pl.multiple_of(owner * frows, frows), frows)]
        return vg.at[pl.ds(pl.multiple_of(owner * vrows + (piece - 1) * half, half), half)]

    def own(piece):
        if piece == 0:
            return f_ref.at[0]
        return v_ref.at[0, pl.ds((piece - 1) * half, half)]

    def across(d, piece):
        return pltpu.make_async_remote_copy(
            src_ref=own(piece), dst_ref=held(piece, col),
            send_sem=gs_send.at[d, piece], recv_sem=gs_recv.at[d, piece],
            device_id={"col": lax.rem(chip + d, chips) * 2 + core}, device_id_type=MESH)

    def onward(d, piece):
        if d == 0:
            source, target = own(piece), held(piece, col)
        else:
            owner = lax.rem(chip + chips - d, chips) * 2 + core
            source = target = held(piece, owner)
        return pltpu.make_async_remote_copy(
            src_ref=source, dst_ref=target,
            send_sem=fw_send.at[d, piece], recv_sem=fw_recv.at[d, piece],
            device_id={"col": partner}, device_id_type=MESH)

    for piece in range(3):
        for d in range(1, chips):
            across(d, piece).start()
        onward(0, piece).start()

    fg[pl.ds(pl.multiple_of(col * frows, frows), frows), :] = f_ref[0]
    vg[pl.ds(pl.multiple_of(col * vrows, vrows), vrows), :] = v_ref[0]
    xt[...] = x_ref[...].T

    for piece in range(3):
        for d in range(1, chips):
            across(d, piece).wait_recv()
            onward(d, piece).start()
        if piece == 0:
            for d in range(chips):
                onward(d, 0).wait_recv()
            f3[...] = as_right(fg[...], 0)
    for piece in (1, 2):
        for d in range(chips):
            onward(d, piece).wait_recv()

    block = band // 4
    blocks = 4

    u3[...] = as_right(vg[:band], 0)

    def make_g(i, _):
        at_row = pl.multiple_of(i * block, block)
        g3[pl.ds(at_row, block), :] = as_right(nn(as_left(vg[pl.ds(at_row, block), :]), f3[...]), 1)
        return 0

    lax.fori_loop(0, blocks, make_g, 0)
    xu3[...] = as_left(nn(as_left(xt[...]), u3[...]))
    at[...] = xt[...] - nt(xu3[...], g3[...])

    def make_c(i, _):
        at_row = pl.multiple_of(i * block, block)
        high, low = halves(-nt(as_left(vg[pl.ds(at_row + band, block), :]), g3[...]))
        ct3[pl.ds(at_row, block), :] = high
        ct3[pl.ds(at_row + band, block), :] = low
        ct3[pl.ds(at_row + 2 * band, block), :] = high
        return 0

    def chain_c():
        lax.fori_loop(0, blocks, make_c, 0)

    def make_h(i, _):
        at_row = pl.multiple_of(i * block, block)
        h3[pl.ds(at_row, block), :] = as_right(nn(as_left(vg[pl.ds(at_row + band, block), :]), f3[...]), 1)
        return 0

    def make_d(i, _):
        at_row = pl.multiple_of(i * block, block)
        high, low = halves(-nt(as_left(vg[pl.ds(at_row + band, block), :]), h3[...]))
        dt3[pl.ds(at_row, block), :] = high
        dt3[pl.ds(at_row + band, block), :] = low
        dt3[pl.ds(at_row + 2 * band, block), :] = high
        return 0

    def chain_d():
        lax.fori_loop(0, blocks, make_h, 0)
        lax.fori_loop(0, blocks, make_d, 0)
        et[...] = -nt(xu3[...], h3[...])

    def down(i):
        return pltpu.make_async_remote_copy(
            src_ref=zout.at[i], dst_ref=zin.at[i], send_sem=z_send.at[i], recv_sem=z_recv.at[i],
            device_id={"row": row - 1}, device_id_type=MESH)

    def back(i):
        return pltpu.make_async_remote_copy(
            src_ref=osend.at[i], dst_ref=ret.at[i], send_sem=o_send.at[i], recv_sem=o_recv.at[i],
            device_id={"row": row + 1}, device_id_type=MESH)

    def rows_of(i):
        return pl.ds(i * part, part)

    @pl.when(last)
    def _():
        for i in range(CHUNKS):
            zout[i] = at[rows_of(i), :]
            down(i).start()

    @pl.when(jnp.logical_not(last))
    def _():
        chain_c()

        @pl.when(row < rows // 2)
        def _():
            chain_d()

    @pl.when(jnp.logical_and(row > 0, jnp.logical_not(last)))
    def _():
        for i in range(CHUNKS):
            down(i).wait_recv()
            zout[i] = at[rows_of(i), :] + nn(as_left(zin[i]), ct3[...])
            down(i).start()

        @pl.when(row >= rows // 2)
        def _():
            chain_d()

        for i in range(CHUNKS):
            osend[i] = zin[i] + et[rows_of(i), :] + nn(as_left(zin[i]), dt3[...])
            back(i).start()

    @pl.when(first)
    def _():
        for i in range(CHUNKS):
            down(i).wait_recv()
            left = as_left(zin[i])
            osend[i] = zin[i] + et[rows_of(i), :] + nn(left, dt3[...])
            back(i).start()
            at[rows_of(i), :] = at[rows_of(i), :] + nn(left, ct3[...])
        out_ref[...] = at[...].T

    @pl.when(row > 0)
    def _():
        for i in range(CHUNKS):
            back(i).wait_recv()
        out_ref[...] = ret[...].reshape(width, band).T
        for i in range(CHUNKS):
            down(i).wait_send()

    @pl.when(jnp.logical_not(last))
    def _():
        for i in range(CHUNKS):
            back(i).wait_send()

    for piece in range(3):
        for d in range(chips):
            if d > 0:
                across(d, piece).wait_send()
            onward(d, piece).wait_send()


def solution(mesh):
    rows, cols = mesh.shape["row"], mesh.shape["col"]
    chips = cols // 2

    def local(vectors, reflectors, factors):
        band, width = vectors.shape
        part = width // CHUNKS
        dma = pltpu.SemaphoreType.DMA
        return pl.pallas_call(
            functools.partial(kernel, rows, cols),
            out_shape=jax.ShapeDtypeStruct((band, width), F32),
            in_specs=[pl.BlockSpec(memory_space=pltpu.VMEM)] * 3,
            out_specs=pl.BlockSpec(memory_space=pltpu.VMEM),
            scratch_shapes=[
                pltpu.VMEM((2 * band, band), F32),
                pltpu.VMEM((band, band), F32),
                pltpu.VMEM((3 * band, band), BF16),
                pltpu.VMEM((3 * band, band), BF16),
                pltpu.VMEM((band, 3 * band), BF16),
                pltpu.VMEM((band, 3 * band), BF16),
                pltpu.VMEM((3 * band, band), BF16),
                pltpu.VMEM((3 * band, band), BF16),
                pltpu.VMEM((width, band), F32),
                pltpu.VMEM((width, band), F32),
                pltpu.VMEM((width, band), F32),
                pltpu.VMEM((width, 3 * band), BF16),
                pltpu.VMEM((CHUNKS, part, band), F32),
                pltpu.VMEM((CHUNKS, part, band), F32),
                pltpu.VMEM((CHUNKS, part, band), F32),
                pltpu.VMEM((CHUNKS, part, band), F32),
                dma((chips, 3)),
                dma((chips, 3)),
                dma((chips, 3)),
                dma((chips, 3)),
                dma((CHUNKS,)),
                dma((CHUNKS,)),
                dma((CHUNKS,)),
                dma((CHUNKS,)),
            ],
            compiler_params=pltpu.CompilerParams(
                collective_id=0, has_side_effects=True, vmem_limit_bytes=40 * 1024 * 1024
            ),
        )(vectors, reflectors, factors)

    in_specs = (P("row", "col"), P("row", "col", None), P("row", "col", None))
    return jax.shard_map(local, mesh=mesh, in_specs=in_specs, out_specs=P("row", "col"), check_vma=False)
```

time: 186 us -> 65.2 us (0.35)
  the two profiles are of different devices: /device:TPU:6 before, /device:TPU:0 now
where the time goes in v1:
time: 65.2 us; the launch traced here: 64.9 us
  Pallas kernels  61.3 us (94%)
  local copies, waits for them, and re-layouts  3.65 us (6%)
    pallas_call x1, Pallas kernels, local(): pl.pallas_call(functools.partial(kernel, rows, cols), out_shape=jax.Shape...  61.3 us
    unnamed x7, local copies, waits for them, and re-layouts  3.65 us

profile of v1, /device:TPU:0, one launch (start us, length us, event | category | flops | bytes accessed | tf_op | source)
XLA Modules:
  0.0 64.9 jit_solution(8802107859077808771)
XLA Ops:
  0.0 0.0 copy-start
  0.0 1.0 %copy-done = f32[1,256,512]{2,1,0:T(8,128)S(1)} copy-done((f32[1,256,512]{2,1,0:T(8,128)S(1)}, f32[1,256,512]{2,1,0:T(8,128)}, u32[]{:S(2)}) %copy-start) | copy-done | bytes 524312
  1.0 0.0 copy-start.1
  1.0 0.9 %copy-done.1 = f32[512,128]{1,0:T(8,128)S(1)} copy-done((f32[512,128]{1,0:T(8,128)S(1)}, f32[512,128]{1,0:T(8,128)}, u32[]{:S(2)}) %copy-start.1) | copy-done | bytes 262168
  2.0 0.0 copy-start.2
  2.0 0.9 %copy-done.2 = f32[1,128,512]{2,1,0:T(8,128)S(1)} copy-done((f32[1,128,512]{2,1,0:T(8,128)S(1)}, f32[1,128,512]{2,1,0:T(8,128)}, u32[]{:S(2)}) %copy-start.2) | copy-done | bytes 262168
  2.9 61.3 %shard_map.37 = f32[512,128]{1,0:T(8,128)S(1)} custom-call(f32[512,128]{1,0:T(8,128)S(1)} %copy-done.1, f32[1,256,512]{2,1,0:T(8,128)S(1)} %copy-done, f32[1,128,512]{2,1,0:T(8,128)S(1)} %copy-done.2), custom_call_target="tpu_custom_call" | custom-call | tf_op jit(solution)/shard_map/pallas_call | solution.py:243
  64.2 0.7 %copy.5 = f32[512,128]{1,0:T(8,128)} copy(f32[512,128]{1,0:T(8,128)S(1)} %shard_map.37) | data formatting | bytes 524288
Async XLA Ops:
  0.0 1.0 %copy-start = (f32[1,256,512]{2,1,0:T(8,128)S(1)}, f32[1,256,512]{2,1,0:T(8,128)}, u32[]{:S(2)}) copy-start(f32[1,256,512]{2,1,0:T(8,128)} %v_ref.1) | copy-start | bytes 1572868
  1.0 0.9 %copy-start.1 = (f32[512,128]{1,0:T(8,128)S(1)}, f32[512,128]{1,0:T(8,128)}, u32[]{:S(2)}) copy-start(f32[512,128]{1,0:T(8,128)} %x_ref.1) | copy-start | bytes 786436
  2.0 0.9 %copy-start.2 = (f32[1,128,512]{2,1,0:T(8,128)S(1)}, f32[1,128,512]{2,1,0:T(8,128)}, u32[]{:S(2)}) copy-start(f32[1,128,512]{2,1,0:T(8,128)} %f_ref.1) | copy-start | bytes 786436

commit v2 on v1

v2 whole, which is shorter than its diff:
```python
import functools

import jax
import jax.numpy as jnp
from jax import lax
from jax.experimental import pallas as pl
from jax.experimental.pallas import tpu as pltpu
from jax.sharding import PartitionSpec as P

MESH = pl.DeviceIdType.MESH
CHUNKS = 4
F32, BF16 = jnp.float32, jnp.bfloat16


def halves(value):
    high = value.astype(BF16)
    return high, (value - high.astype(F32)).astype(BF16)


def dot(left, right, axis):
    return lax.dot_general(left, right, (((1,), (axis,)), ((), ())), preferred_element_type=F32)


def product(left, high, low, axis):
    left_high, left_low = halves(left)
    return dot(left_high, high, axis) + (dot(left_high, low, axis) + dot(left_low, high, axis))


def kernel(rows, cols, x_ref, v_ref, f_ref, out_ref,
           xs, vg, fg, vh, vl, fh, fl, mg, kg, ch, cl, dh, dl, at, et, xt, qt, zin, zout, osend, ret,
           load_sem, gs_send, gs_recv, fw_send, fw_recv, z_send, z_recv, o_send, o_recv):
    row, col = lax.axis_index("row"), lax.axis_index("col")
    chips = cols // 2
    side = chips // 2
    core, chip = lax.rem(col, 2), col // 2
    partner = chip * 2 + (1 - core)
    band = fg.shape[0]
    vrows, frows = v_ref.shape[1], f_ref.shape[1]
    half = vrows // 2
    width = xt.shape[0]
    part = width // CHUNKS
    first, last = row == 0, row == rows - 1
    holds_upper = chip < side
    near_base = jnp.where(holds_upper, 0, side)
    far_base = side - near_base
    place = chip - near_base

    def chip_at(d, sign):
        base = near_base if d < side else far_base
        return base + lax.rem(place + side + sign * (d % side), side)

    barrier = pltpu.get_barrier_semaphore()

    def greet(device):
        pl.semaphore_signal(barrier, inc=1, device_id=device, device_id_type=MESH)

    greet({"col": partner})
    for d in range(1, chips):
        greet({"col": chip_at(d, 1) * 2 + core})

    @pl.when(row > 0)
    def _():
        greet({"row": row - 1})

    @pl.when(row < rows - 1)
    def _():
        greet({"row": row + 1})

    own_f = fg.at[pl.ds(pl.multiple_of(col * frows, frows), frows)]
    own_v = vg.at[pl.ds(pl.multiple_of(col * vrows, vrows), vrows)]
    loads = (pltpu.make_async_copy(v_ref.at[0], own_v, load_sem.at[0]),
             pltpu.make_async_copy(f_ref.at[0], own_f, load_sem.at[1]),
             pltpu.make_async_copy(x_ref, xs, load_sem.at[2]))
    for load in loads:
        load.start()

    edges = jnp.where(first, 0, 1) + jnp.where(last, 0, 1)
    pl.semaphore_wait(barrier, chips + edges)

    def row_of(piece, owner):
        return pl.multiple_of(owner * vrows + (piece - 1) * half, half)

    def held(piece, owner):
        if piece == 0:
            return fg.at[pl.ds(pl.multiple_of(owner * frows, frows), frows)]
        return vg.at[pl.ds(row_of(piece, owner), half)]

    def own(piece):
        if piece == 0:
            return f_ref.at[0]
        return v_ref.at[0, pl.ds((piece - 1) * half, half)]

    def across(d, piece):
        return pltpu.make_async_remote_copy(
            src_ref=own(piece), dst_ref=held(piece, col),
            send_sem=gs_send.at[d, piece], recv_sem=gs_recv.at[d, piece],
            device_id={"col": chip_at(d, 1) * 2 + core}, device_id_type=MESH)

    def onward(d, piece):
        owner = chip_at(d, -1) * 2 + core
        return pltpu.make_async_remote_copy(
            src_ref=own(piece) if d == 0 else held(piece, owner), dst_ref=held(piece, owner),
            send_sem=fw_send.at[d, piece], recv_sem=fw_recv.at[d, piece],
            device_id={"col": partner}, device_id_type=MESH)

    for piece in range(3):
        for d in range(1, chips):
            across(d, piece).start()
    for piece in (1, 2, 0):
        onward(0, piece).start()

    def down(i):
        return pltpu.make_async_remote_copy(
            src_ref=zout.at[i], dst_ref=zin.at[i], send_sem=z_send.at[i], recv_sem=z_recv.at[i],
            device_id={"row": row - 1}, device_id_type=MESH)

    def back(i):
        return pltpu.make_async_remote_copy(
            src_ref=osend.at[i], dst_ref=ret.at[i], send_sem=o_send.at[i], recv_sem=o_recv.at[i],
            device_id={"row": row + 1}, device_id_type=MESH)

    def rows_of(i):
        return pl.ds(i * part, part)

    block = band // 4

    def over_blocks(step):
        def body(i, _):
            step(pl.multiple_of(i * block, block))
            return 0

        lax.fori_loop(0, 4, body, 0)

    def split_rows(start):
        span = pl.ds(start, block)
        vh[span, :], vl[span, :] = halves(vg[span, :])

    upper, lower = pl.ds(0, band), pl.ds(band, band)

    for load in loads:
        load.wait()
    xt[...] = xs[...].T

    for piece in (1, 2):
        for d in range(1, side):
            across(d, piece).wait_recv()
            onward(d, piece).start()
        for d in range(side):
            onward(d, piece).wait_recv()
    near_row = jnp.where(holds_upper, 0, band)
    over_blocks(lambda start: split_rows(pl.multiple_of(near_row + start, block)))

    def make_xu():
        qt[...] = product(xt[...], vh[upper, :], vl[upper, :], 0)

    def make_a():
        q = product(qt[...], fh[...], fl[...], 1)
        qt[...] = q
        at[...] = xt[...] - product(q, vh[upper, :], vl[upper, :], 1)

        @pl.when(last)
        def _():
            for i in range(CHUNKS):
                zout[i] = at[rows_of(i), :]
                down(i).start()

    @pl.when(holds_upper)
    def _():
        make_xu()

    for d in range(1, chips):
        across(d, 0).wait_recv()
        onward(d, 0).start()
    for d in range(chips):
        onward(d, 0).wait_recv()

    def split_f(start):
        span = pl.ds(start, block)
        fh[span, :], fl[span, :] = halves(fg[span, :])

    over_blocks(split_f)

    def make_g(start):
        span = pl.ds(start, block)
        mg[0, span, :], mg[1, span, :] = halves(product(vg[span, :], fh[...], fl[...], 0))

    def make_k(start):
        span = pl.ds(start, block)
        k = product(vg[pl.ds(pl.multiple_of(band + start, block), block), :], fh[...], fl[...], 1)
        kg[span, :] = k

    @pl.when(holds_upper)
    def _():
        make_a()
        over_blocks(make_g)

    @pl.when(jnp.logical_not(holds_upper))
    def _():
        over_blocks(make_k)

    def use_far(start):
        split_rows(start)

        @pl.when(jnp.logical_and(holds_upper, jnp.logical_not(last)))
        def _():
            span = pl.ds(pl.multiple_of(start - band, block), block)
            ch[span, :], cl[span, :] = halves(-product(vg[pl.ds(start, block), :], mg[0], mg[1], 1))

        @pl.when(jnp.logical_and(jnp.logical_not(holds_upper), jnp.logical_not(last)))
        def _():
            span = pl.ds(start, block)
            ch[:, span], cl[:, span] = halves(-product(kg[...], vh[span, :], vl[span, :], 1))

    def far_start(piece, owner):
        return pl.multiple_of(owner * vrows + (piece - 1) * half, block)

    fine = half == block
    for piece in (1, 2):
        for d in range(side, chips):
            across(d, piece).wait_recv()
            onward(d, piece).start()
        if fine:
            for d in range(side, chips):
                use_far(far_start(piece, chip_at(d, -1) * 2 + core))
        for d in range(side, chips):
            onward(d, piece).wait_recv()
        if fine:
            for d in range(side, chips):
                use_far(far_start(piece, chip_at(d, -1) * 2 + 1 - core))
    if not fine:
        over_blocks(lambda start: use_far(pl.multiple_of(band - near_row + start, block)))

    @pl.when(jnp.logical_not(holds_upper))
    def _():
        make_xu()
        make_a()

    def make_d(start):
        span = pl.ds(start, block)
        dh[span, :], dl[span, :] = halves(-product(kg[span, :], vh[lower, :], vl[lower, :], 1))

    def chain_d():
        @pl.when(holds_upper)
        def _():
            over_blocks(make_k)

        over_blocks(make_d)
        et[...] = -product(qt[...], vh[lower, :], vl[lower, :], 1)

    @pl.when(row < rows // 2)
    def _():
        chain_d()

    @pl.when(jnp.logical_and(row > 0, jnp.logical_not(last)))
    def _():
        for i in range(CHUNKS):
            down(i).wait_recv()
            zout[i] = at[rows_of(i), :] + product(zin[i], ch[...], cl[...], 0)
            down(i).start()

        @pl.when(row >= rows // 2)
        def _():
            chain_d()

        for i in range(CHUNKS):
            osend[i] = zin[i] + et[rows_of(i), :] + product(zin[i], dh[...], dl[...], 0)
            back(i).start()

    @pl.when(first)
    def _():
        for i in range(CHUNKS):
            down(i).wait_recv()
            osend[i] = zin[i] + et[rows_of(i), :] + product(zin[i], dh[...], dl[...], 0)
            back(i).start()
            at[rows_of(i), :] = at[rows_of(i), :] + product(zin[i], ch[...], cl[...], 0)
        out_ref[...] = at[...].T

    @pl.when(row > 0)
    def _():
        for i in range(CHUNKS):
            back(i).wait_recv()
        out_ref[...] = ret[...].reshape(width, band).T
        for i in range(CHUNKS):
            down(i).wait_send()

    @pl.when(jnp.logical_not(last))
    def _():
        for i in range(CHUNKS):
            back(i).wait_send()

    for piece in range(3):
        for d in range(chips):
            if d > 0:
                across(d, piece).wait_send()
            onward(d, piece).wait_send()


def solution(mesh):
    rows, cols = mesh.shape["row"], mesh.shape["col"]
    chips = cols // 2

    def local(vectors, reflectors, factors):
        band, width = vectors.shape
        part = width // CHUNKS
        dma = pltpu.SemaphoreType.DMA
        return pl.pallas_call(
            functools.partial(kernel, rows, cols),
            out_shape=jax.ShapeDtypeStruct((band, width), F32),
            in_specs=[pl.BlockSpec(memory_space=pl.ANY)] * 3,
            out_specs=pl.BlockSpec(memory_space=pltpu.VMEM),
            scratch_shapes=[
                pltpu.VMEM((band, width), F32),
                pltpu.VMEM((2 * band, band), F32),
                pltpu.VMEM((band, band), F32),
                pltpu.VMEM((2 * band, band), BF16),
                pltpu.VMEM((2 * band, band), BF16),
                pltpu.VMEM((band, band), BF16),
                pltpu.VMEM((band, band), BF16),
                pltpu.VMEM((2, band, band), BF16),
                pltpu.VMEM((band, band), F32),
                pltpu.VMEM((band, band), BF16),
                pltpu.VMEM((band, band), BF16),
                pltpu.VMEM((band, band), BF16),
                pltpu.VMEM((band, band), BF16),
                pltpu.VMEM((width, band), F32),
                pltpu.VMEM((width, band), F32),
                pltpu.VMEM((width, band), F32),
                pltpu.VMEM((width, band), F32),
                pltpu.VMEM((CHUNKS, part, band), F32),
                pltpu.VMEM((CHUNKS, part, band), F32),
                pltpu.VMEM((CHUNKS, part, band), F32),
                pltpu.VMEM((CHUNKS, part, band), F32),
                dma((3,)),
                dma((chips, 3)),
                dma((chips, 3)),
                dma((chips, 3)),
                dma((chips, 3)),
                dma((CHUNKS,)),
                dma((CHUNKS,)),
                dma((CHUNKS,)),
                dma((CHUNKS,)),
            ],
            compiler_params=pltpu.CompilerParams(
                collective_id=0, has_side_effects=True, vmem_limit_bytes=56 * 1024 * 1024
            ),
        )(vectors, reflectors, factors)

    in_specs = (P("row", "col"), P("row", "col", None), P("row", "col", None))
    return jax.shard_map(local, mesh=mesh, in_specs=in_specs, out_specs=P("row", "col"), check_vma=False)
```

time: 65.2 us -> 61.1 us (0.937)
  the two profiles are of different devices: /device:TPU:0 before, /device:TPU:6 now
where the time goes in v2:
time: 61.1 us; the launch traced here: 61 us
  Pallas kernels  59.3 us (97%)
  local copies, waits for them, and re-layouts  1.67 us (3%)
    pallas_call x1, Pallas kernels, local(): pl.pallas_call(functools.partial(kernel, rows, cols), out_shape=jax.Shape...  59.3 us
    unnamed x1, local copies, waits for them, and re-layouts  1.67 us

profile of v2, /device:TPU:6, one launch (start us, length us, event | category | flops | bytes accessed | tf_op | source)
XLA Modules:
  0.0 61.0 jit_solution(11792799300407487272)
XLA Ops:
  0.0 59.3 %shard_map.37 = f32[512,128]{1,0:T(8,128)} custom-call(f32[512,128]{1,0:T(8,128)} %x_ref.1, f32[1,256,512]{2,1,0:T(8,128)} %v_ref.1, f32[1,128,512]{2,1,0:T(8,128)} %f_ref.1), custom_call_target="tpu_custom_call" | custom-call | tf_op jit(solution)/shard_map/pallas_call | solution.py:306
  59.3 1.7 %copy.5 = f32[512,128]{1,0:T(8,128)} copy(f32[512,128]{1,0:T(8,128)} %shard_map.37) | data formatting | bytes 524288

commit v3 on v2

--- a/solution.py
+++ b/solution.py
@@ -8,7 +8,7 @@
 from jax.sharding import PartitionSpec as P
 
 MESH = pl.DeviceIdType.MESH
-CHUNKS = 4
+CHUNKS = 8
 F32, BF16 = jnp.float32, jnp.bfloat16
 
 
@@ -22,7 +22,10 @@
 
 
 def product(left, high, low, axis):
-    left_high, left_low = halves(left)
+    return split_product(*halves(left), high, low, axis)
+
+
+def split_product(left_high, left_low, high, low, axis):
     return dot(left_high, high, axis) + (dot(left_high, low, axis) + dot(left_low, high, axis))
 
 
@@ -186,8 +189,8 @@
 
     def make_k(start):
         span = pl.ds(start, block)
-        k = product(vg[pl.ds(pl.multiple_of(band + start, block), block), :], fh[...], fl[...], 1)
-        kg[span, :] = k
+        left = vg[pl.ds(pl.multiple_of(band + start, block), block), :]
+        kg[0, span, :], kg[1, span, :] = halves(product(left, fh[...], fl[...], 1))
 
     @pl.when(holds_upper)
     def _():
@@ -209,7 +212,7 @@
         @pl.when(jnp.logical_and(jnp.logical_not(holds_upper), jnp.logical_not(last)))
         def _():
             span = pl.ds(start, block)
-            ch[:, span], cl[:, span] = halves(-product(kg[...], vh[span, :], vl[span, :], 1))
+            ch[:, span], cl[:, span] = halves(-split_product(kg[0], kg[1], vh[span, :], vl[span, :], 1))
 
     def far_start(piece, owner):
         return pl.multiple_of(owner * vrows + (piece - 1) * half, block)
@@ -237,7 +240,8 @@
 
     def make_d(start):
         span = pl.ds(start, block)
-        dh[span, :], dl[span, :] = halves(-product(kg[span, :], vh[lower, :], vl[lower, :], 1))
+        dh[span, :], dl[span, :] = halves(
+            -split_product(kg[0, span, :], kg[1, span, :], vh[lower, :], vl[lower, :], 1))
 
     def chain_d():
         @pl.when(holds_upper)
@@ -247,31 +251,38 @@
         over_blocks(make_d)
         et[...] = -product(qt[...], vh[lower, :], vl[lower, :], 1)
 
+    def hop(i):
+        down(i).wait_recv()
+        zout[i] = at[rows_of(i), :] + product(zin[i], ch[...], cl[...], 0)
+        down(i).start()
+
+    def give_back(i):
+        osend[i] = zin[i] + et[rows_of(i), :] + product(zin[i], dh[...], dl[...], 0)
+        back(i).start()
+
+    @pl.when(jnp.logical_and(row >= rows // 2, jnp.logical_not(last)))
+    def _():
+        for i in range(CHUNKS):
+            hop(i)
+        chain_d()
+        for i in range(CHUNKS):
+            give_back(i)
+
     @pl.when(row < rows // 2)
     def _():
         chain_d()
 
-    @pl.when(jnp.logical_and(row > 0, jnp.logical_not(last)))
+    @pl.when(jnp.logical_and(row < rows // 2, row > 0))
+    def _():
+        for i in range(CHUNKS):
+            hop(i)
+            give_back(i)
+
+    @pl.when(first)
     def _():
         for i in range(CHUNKS):
             down(i).wait_recv()
-            zout[i] = at[rows_of(i), :] + product(zin[i], ch[...], cl[...], 0)
-            down(i).start()
-
-        @pl.when(row >= rows // 2)
-        def _():
-            chain_d()
-
-        for i in range(CHUNKS):
-            osend[i] = zin[i] + et[rows_of(i), :] + product(zin[i], dh[...], dl[...], 0)
-            back(i).start()
-
-    @pl.when(first)
-    def _():
-        for i in range(CHUNKS):
-            down(i).wait_recv()
-            osend[i] = zin[i] + et[rows_of(i), :] + product(zin[i], dh[...], dl[...], 0)
-            back(i).start()
+            give_back(i)
             at[rows_of(i), :] = at[rows_of(i), :] + product(zin[i], ch[...], cl[...], 0)
         out_ref[...] = at[...].T
 
@@ -317,7 +328,7 @@
                 pltpu.VMEM((band, band), BF16),
                 pltpu.VMEM((band, band), BF16),
                 pltpu.VMEM((2, band, band), BF16),
-                pltpu.VMEM((band, band), F32),
+                pltpu.VMEM((2, band, band), BF16),
                 pltpu.VMEM((band, band), BF16),
                 pltpu.VMEM((band, band), BF16),
                 pltpu.VMEM((band, band), BF16),

time: 61.1 us -> 58.8 us (0.962)
  Pallas kernels: 59.3 us -> 57 us
    pallas_call x1, Pallas kernels: 59.3 us -> 57 us  [local(): pl.pallas_call(functools.partial(kernel, rows, cols), out_shape=jax.Shape...]
where the time goes in v3:
time: 58.8 us; the launch traced here: 58.7 us
  Pallas kernels  57 us (97%)
  local copies, waits for them, and re-layouts  1.67 us (3%)
    pallas_call x1, Pallas kernels, local(): pl.pallas_call(functools.partial(kernel, rows, cols), out_shape=jax.Shape...  57 us
    unnamed x1, local copies, waits for them, and re-layouts  1.67 us

profile of v3, /device:TPU:6, one launch (start us, length us, event | category | flops | bytes accessed | tf_op | source)
XLA Modules:
  0.0 58.7 jit_solution(607449910495114525)
XLA Ops:
  0.0 57.0 %shard_map.37 = f32[512,128]{1,0:T(8,128)} custom-call(f32[512,128]{1,0:T(8,128)} %x_ref.1, f32[1,256,512]{2,1,0:T(8,128)} %v_ref.1, f32[1,128,512]{2,1,0:T(8,128)} %f_ref.1), custom_call_target="tpu_custom_call" | custom-call | tf_op jit(solution)/shard_map/pallas_call | solution.py:317
  57.0 1.7 %copy.5 = f32[512,128]{1,0:T(8,128)} copy(f32[512,128]{1,0:T(8,128)} %shard_map.37) | data formatting | bytes 524288

commit v4 on v3

--- a/solution.py
+++ b/solution.py
@@ -26,12 +26,14 @@
 
 
 def split_product(left_high, left_low, high, low, axis):
-    return dot(left_high, high, axis) + (dot(left_high, low, axis) + dot(left_low, high, axis))
+    both = dot(jnp.concatenate([left_high, left_low], axis=0), high, axis)
+    count = left_high.shape[0]
+    return both[:count] + (both[count:] + dot(left_high, low, axis))
 
 
 def kernel(rows, cols, x_ref, v_ref, f_ref, out_ref,
-           xs, vg, fg, vh, vl, fh, fl, mg, kg, ch, cl, dh, dl, at, et, xt, qt, zin, zout, osend, ret,
-           load_sem, gs_send, gs_recv, fw_send, fw_recv, z_send, z_recv, o_send, o_recv):
+           xs, xm, zm, vg, fg, vh, vl, fh, fl, mg, kg, ch, cl, dh, dl, at, et, xt, qt, zin, zout, osend, ret,
+           load_sem, gs_send, gs_recv, fw_send, fw_recv, z_send, z_recv, o_send, o_recv, x_send, x_recv, m_send):
     row, col = lax.axis_index("row"), lax.axis_index("col")
     chips = cols // 2
     side = chips // 2
@@ -69,6 +71,18 @@
     def _():
         greet({"row": row + 1})
 
+    mate = chip_at(side, 1) * 2 + core
+    above_mate = {"row": row - 1, "col": mate}
+    lends, borrows = jnp.logical_and(last, holds_upper), jnp.logical_and(row == rows - 2, jnp.logical_not(holds_upper))
+
+    @pl.when(lends)
+    def _():
+        greet(above_mate)
+
+    @pl.when(borrows)
+    def _():
+        greet({"row": row + 1, "col": mate})
+
     own_f = fg.at[pl.ds(pl.multiple_of(col * frows, frows), frows)]
     own_v = vg.at[pl.ds(pl.multiple_of(col * vrows, vrows), vrows)]
     loads = (pltpu.make_async_copy(v_ref.at[0], own_v, load_sem.at[0]),
@@ -77,7 +91,7 @@
     for load in loads:
         load.start()
 
-    edges = jnp.where(first, 0, 1) + jnp.where(last, 0, 1)
+    edges = jnp.where(first, 0, 1) + jnp.where(last, 0, 1) + jnp.where(lends, 1, 0) + jnp.where(borrows, 1, 0)
     pl.semaphore_wait(barrier, chips + edges)
 
     def row_of(piece, owner):
@@ -106,9 +120,17 @@
             send_sem=fw_send.at[d, piece], recv_sem=fw_recv.at[d, piece],
             device_id={"col": partner}, device_id_type=MESH)
 
+    move_x = pltpu.make_async_remote_copy(
+        src_ref=x_ref, dst_ref=xm, send_sem=x_send, recv_sem=x_recv,
+        device_id={"col": mate}, device_id_type=MESH)
+
     for piece in range(3):
         for d in range(1, chips):
             across(d, piece).start()
+        if piece == 0:
+            @pl.when(jnp.logical_and(last, jnp.logical_not(holds_upper)))
+            def _():
+                move_x.start()
     for piece in (1, 2, 0):
         onward(0, piece).start()
 
@@ -116,6 +138,11 @@
         return pltpu.make_async_remote_copy(
             src_ref=zout.at[i], dst_ref=zin.at[i], send_sem=z_send.at[i], recv_sem=z_recv.at[i],
             device_id={"row": row - 1}, device_id_type=MESH)
+
+    def down_mate(i):
+        return pltpu.make_async_remote_copy(
+            src_ref=zm.at[i], dst_ref=zin.at[i], send_sem=m_send.at[i], recv_sem=z_recv.at[i],
+            device_id=above_mate, device_id_type=MESH)
 
     def back(i):
         return pltpu.make_async_remote_copy(
@@ -153,23 +180,17 @@
     near_row = jnp.where(holds_upper, 0, band)
     over_blocks(lambda start: split_rows(pl.multiple_of(near_row + start, block)))
 
-    def make_xu():
-        qt[...] = product(xt[...], vh[upper, :], vl[upper, :], 0)
-
-    def make_a():
+    def make_xu(x):
+        qt[...] = product(x, vh[upper, :], vl[upper, :], 0)
+
+    def make_a(x):
         q = product(qt[...], fh[...], fl[...], 1)
         qt[...] = q
-        at[...] = xt[...] - product(q, vh[upper, :], vl[upper, :], 1)
-
-        @pl.when(last)
-        def _():
-            for i in range(CHUNKS):
-                zout[i] = at[rows_of(i), :]
-                down(i).start()
+        at[...] = x - product(q, vh[upper, :], vl[upper, :], 1)
 
     @pl.when(holds_upper)
     def _():
-        make_xu()
+        make_xu(xt[...])
 
     for d in range(1, chips):
         across(d, 0).wait_recv()
@@ -194,10 +215,26 @@
 
     @pl.when(holds_upper)
     def _():
-        make_a()
-        over_blocks(make_g)
-
-    @pl.when(jnp.logical_not(holds_upper))
+        make_a(xt[...])
+
+        @pl.when(jnp.logical_not(last))
+        def _():
+            over_blocks(make_g)
+
+    @pl.when(lends)
+    def _():
+        for i in range(CHUNKS):
+            zout[i] = at[rows_of(i), :]
+            down(i).start()
+        move_x.wait_recv()
+        xt[...] = xm[...].T
+        make_xu(xt[...])
+        make_a(xt[...])
+        for i in range(CHUNKS):
+            zm[i] = at[rows_of(i), :]
+            down_mate(i).start()
+
+    @pl.when(jnp.logical_not(jnp.logical_or(holds_upper, last)))
     def _():
         over_blocks(make_k)
 
@@ -233,10 +270,10 @@
     if not fine:
         over_blocks(lambda start: use_far(pl.multiple_of(band - near_row + start, block)))
 
-    @pl.when(jnp.logical_not(holds_upper))
-    def _():
-        make_xu()
-        make_a()
+    @pl.when(jnp.logical_not(jnp.logical_or(holds_upper, last)))
+    def _():
+        make_xu(xt[...])
+        make_a(xt[...])
 
     def make_d(start):
         span = pl.ds(start, block)
@@ -291,8 +328,20 @@
         for i in range(CHUNKS):
             back(i).wait_recv()
         out_ref[...] = ret[...].reshape(width, band).T
+
+    @pl.when(jnp.logical_and(row > 0, jnp.logical_or(holds_upper, row < rows - 1)))
+    def _():
         for i in range(CHUNKS):
             down(i).wait_send()
+
+    @pl.when(lends)
+    def _():
+        for i in range(CHUNKS):
+            down_mate(i).wait_send()
+
+    @pl.when(jnp.logical_and(last, jnp.logical_not(holds_upper)))
+    def _():
+        move_x.wait_send()
 
     @pl.when(jnp.logical_not(last))
     def _():
@@ -321,6 +370,8 @@
             out_specs=pl.BlockSpec(memory_space=pltpu.VMEM),
             scratch_shapes=[
                 pltpu.VMEM((band, width), F32),
+                pltpu.VMEM((band, width), F32),
+                pltpu.VMEM((CHUNKS, part, band), F32),
                 pltpu.VMEM((2 * band, band), F32),
                 pltpu.VMEM((band, band), F32),
                 pltpu.VMEM((2 * band, band), BF16),
@@ -350,6 +401,9 @@
                 dma((CHUNKS,)),
                 dma((CHUNKS,)),
                 dma((CHUNKS,)),
+                dma,
+                dma,
+                dma((CHUNKS,)),
             ],
             compiler_params=pltpu.CompilerParams(
                 collective_id=0, has_side_effects=True, vmem_limit_bytes=56 * 1024 * 1024

time: 58.8 us -> 56.1 us (0.954)
  Pallas kernels: 57 us -> 54.3 us
    pallas_call x1, Pallas kernels: 57 us -> 54.3 us  [local(): pl.pallas_call(functools.partial(kernel, rows, cols), out_shape=jax.Shape...]
where the time goes in v4:
time: 56.1 us; the launch traced here: 56 us
  Pallas kernels  54.3 us (97%)
  local copies, waits for them, and re-layouts  1.67 us (3%)
    pallas_call x1, Pallas kernels, local(): pl.pallas_call(functools.partial(kernel, rows, cols), out_shape=jax.Shape...  54.3 us
    unnamed x1, local copies, waits for them, and re-layouts  1.67 us

profile of v4, /device:TPU:6, one launch (start us, length us, event | category | flops | bytes accessed | tf_op | source)
XLA Modules:
  0.0 56.0 jit_solution(1638272516789426804)
XLA Ops:
  0.0 54.3 %shard_map.37 = f32[512,128]{1,0:T(8,128)} custom-call(f32[512,128]{1,0:T(8,128)} %x_ref.1, f32[1,256,512]{2,1,0:T(8,128)} %v_ref.1, f32[1,128,512]{2,1,0:T(8,128)} %f_ref.1), custom_call_target="tpu_custom_call" | custom-call | tf_op jit(solution)/shard_map/pallas_call | solution.py:366
  54.3 1.7 %copy.5 = f32[512,128]{1,0:T(8,128)} copy(f32[512,128]{1,0:T(8,128)} %shard_map.37) | data formatting | bytes 524288

commit v5 on v4

--- a/solution.py
+++ b/solution.py
@@ -297,19 +297,23 @@
         osend[i] = zin[i] + et[rows_of(i), :] + product(zin[i], dh[...], dl[...], 0)
         back(i).start()
 
-    @pl.when(jnp.logical_and(row >= rows // 2, jnp.logical_not(last)))
+    @pl.when(row < rows // 2)
+    def _():
+        chain_d()
+
+    @pl.when(jnp.logical_and(row > 1, jnp.logical_not(last)))
     def _():
         for i in range(CHUNKS):
             hop(i)
-        chain_d()
+
+        @pl.when(row >= rows // 2)
+        def _():
+            chain_d()
+
         for i in range(CHUNKS):
             give_back(i)
 
-    @pl.when(row < rows // 2)
-    def _():
-        chain_d()
-
-    @pl.when(jnp.logical_and(row < rows // 2, row > 0))
+    @pl.when(row == 1)
     def _():
         for i in range(CHUNKS):
             hop(i)

time: 56.1 us -> 56.1 us (level)
  no operation moved by 1% of the time
where the time goes in v5:
time: 56.1 us; the launch traced here: 55.9 us
  Pallas kernels  54.2 us (97%)
  local copies, waits for them, and re-layouts  1.67 us (3%)
    pallas_call x1, Pallas kernels, local(): pl.pallas_call(functools.partial(kernel, rows, cols), out_shape=jax.Shape...  54.2 us
    unnamed x1, local copies, waits for them, and re-layouts  1.67 us

profile of v5, /device:TPU:6, one launch (start us, length us, event | category | flops | bytes accessed | tf_op | source)
XLA Modules:
  0.0 55.9 jit_solution(15999486546002959163)
XLA Ops:
  0.0 54.2 %shard_map.37 = f32[512,128]{1,0:T(8,128)} custom-call(f32[512,128]{1,0:T(8,128)} %x_ref.1, f32[1,256,512]{2,1,0:T(8,128)} %v_ref.1, f32[1,128,512]{2,1,0:T(8,128)} %f_ref.1), custom_call_target="tpu_custom_call" | custom-call | tf_op jit(solution)/shard_map/pallas_call | solution.py:370
  54.3 1.7 %copy.5 = f32[512,128]{1,0:T(8,128)} copy(f32[512,128]{1,0:T(8,128)} %shard_map.37) | data formatting | bytes 524288

commit v6 on v5

--- a/solution.py
+++ b/solution.py
@@ -134,23 +134,27 @@
     for piece in (1, 2, 0):
         onward(0, piece).start()
 
-    def down(i):
+    def down(i, h):
         return pltpu.make_async_remote_copy(
-            src_ref=zout.at[i], dst_ref=zin.at[i], send_sem=z_send.at[i], recv_sem=z_recv.at[i],
+            src_ref=zout.at[i, h], dst_ref=zin.at[i, h], send_sem=z_send.at[i, h], recv_sem=z_recv.at[i, h],
             device_id={"row": row - 1}, device_id_type=MESH)
 
-    def down_mate(i):
+    def down_mate(i, h):
         return pltpu.make_async_remote_copy(
-            src_ref=zm.at[i], dst_ref=zin.at[i], send_sem=m_send.at[i], recv_sem=z_recv.at[i],
+            src_ref=zm.at[i, h], dst_ref=zin.at[i, h], send_sem=m_send.at[i, h], recv_sem=z_recv.at[i, h],
             device_id=above_mate, device_id_type=MESH)
 
-    def back(i):
+    def back(i, h):
         return pltpu.make_async_remote_copy(
-            src_ref=osend.at[i], dst_ref=ret.at[i], send_sem=o_send.at[i], recv_sem=o_recv.at[i],
+            src_ref=osend.at[i, h], dst_ref=ret.at[i, h], send_sem=o_send.at[i, h], recv_sem=o_recv.at[i, h],
             device_id={"row": row + 1}, device_id_type=MESH)
 
     def rows_of(i):
         return pl.ds(i * part, part)
+
+    wide = band // 2
+    both = (0, 1)
+    span_of = (pl.ds(0, wide), pl.ds(wide, wide))
 
     block = band // 4
 
@@ -224,15 +228,17 @@
     @pl.when(lends)
     def _():
         for i in range(CHUNKS):
-            zout[i] = at[rows_of(i), :]
-            down(i).start()
+            for h in both:
+                zout[i, h] = at[rows_of(i), span_of[h]]
+                down(i, h).start()
         move_x.wait_recv()
         xt[...] = xm[...].T
         make_xu(xt[...])
         make_a(xt[...])
         for i in range(CHUNKS):
-            zm[i] = at[rows_of(i), :]
-            down_mate(i).start()
+            for h in both:
+                zm[i, h] = at[rows_of(i), span_of[h]]
+                down_mate(i, h).start()
 
     @pl.when(jnp.logical_not(jnp.logical_or(holds_upper, last)))
     def _():
@@ -288,14 +294,31 @@
         over_blocks(make_d)
         et[...] = -product(qt[...], vh[lower, :], vl[lower, :], 1)
 
-    def hop(i):
-        down(i).wait_recv()
-        zout[i] = at[rows_of(i), :] + product(zin[i], ch[...], cl[...], 0)
-        down(i).start()
+    def along(left, high, low, k, n):
+        return split_product(*left, high[span_of[k], span_of[n]], low[span_of[k], span_of[n]], 0)
+
+    def hop(i, emit):
+        down(i, 0).wait_recv()
+        left = halves(zin[i, 0])
+        begun = [at[rows_of(i), span_of[n]] + along(left, ch, cl, 0, n) for n in both]
+        down(i, 1).wait_recv()
+        left = halves(zin[i, 1])
+        for n in both:
+            emit(n, begun[n] + along(left, ch, cl, 1, n))
+
+    def pass_on(i):
+        def emit(n, value):
+            zout[i, n] = value
+            down(i, n).start()
+
+        hop(i, emit)
 
     def give_back(i):
-        osend[i] = zin[i] + et[rows_of(i), :] + product(zin[i], dh[...], dl[...], 0)
-        back(i).start()
+        lefts = [halves(zin[i, k]) for k in both]
+        for n in both:
+            osend[i, n] = (zin[i, n] + et[rows_of(i), span_of[n]]
+                           + along(lefts[0], dh, dl, 0, n) + along(lefts[1], dh, dl, 1, n))
+            back(i, n).start()
 
     @pl.when(row < rows // 2)
     def _():
@@ -304,7 +327,7 @@
     @pl.when(jnp.logical_and(row > 1, jnp.logical_not(last)))
     def _():
         for i in range(CHUNKS):
-            hop(i)
+            pass_on(i)
 
         @pl.when(row >= rows // 2)
         def _():
@@ -316,32 +339,40 @@
     @pl.when(row == 1)
     def _():
         for i in range(CHUNKS):
-            hop(i)
+            pass_on(i)
             give_back(i)
 
     @pl.when(first)
     def _():
         for i in range(CHUNKS):
-            down(i).wait_recv()
+            for h in both:
+                down(i, h).wait_recv()
             give_back(i)
-            at[rows_of(i), :] = at[rows_of(i), :] + product(zin[i], ch[...], cl[...], 0)
+            lefts = [halves(zin[i, k]) for k in both]
+            for n in both:
+                at[rows_of(i), span_of[n]] = (at[rows_of(i), span_of[n]]
+                                              + along(lefts[0], ch, cl, 0, n) + along(lefts[1], ch, cl, 1, n))
         out_ref[...] = at[...].T
 
     @pl.when(row > 0)
     def _():
         for i in range(CHUNKS):
-            back(i).wait_recv()
-        out_ref[...] = ret[...].reshape(width, band).T
+            for h in both:
+                back(i, h).wait_recv()
+        for h in both:
+            out_ref[span_of[h], :] = ret[:, h].reshape(width, wide).T
 
     @pl.when(jnp.logical_and(row > 0, jnp.logical_or(holds_upper, row < rows - 1)))
     def _():
         for i in range(CHUNKS):
-            down(i).wait_send()
+            for h in both:
+                down(i, h).wait_send()
 
     @pl.when(lends)
     def _():
         for i in range(CHUNKS):
-            down_mate(i).wait_send()
+            for h in both:
+                down_mate(i, h).wait_send()
 
     @pl.when(jnp.logical_and(last, jnp.logical_not(holds_upper)))
     def _():
@@ -350,7 +381,8 @@
     @pl.when(jnp.logical_not(last))
     def _():
         for i in range(CHUNKS):
-            back(i).wait_send()
+            for h in both:
+                back(i, h).wait_send()
 
     for piece in range(3):
         for d in range(chips):
@@ -375,7 +407,7 @@
             scratch_shapes=[
                 pltpu.VMEM((band, width), F32),
                 pltpu.VMEM((band, width), F32),
-                pltpu.VMEM((CHUNKS, part, band), F32),
+                pltpu.VMEM((CHUNKS, 2, part, band // 2), F32),
                 pltpu.VMEM((2 * band, band), F32),
                 pltpu.VMEM((band, band), F32),
                 pltpu.VMEM((2 * band, band), BF16),
@@ -392,22 +424,22 @@
                 pltpu.VMEM((width, band), F32),
                 pltpu.VMEM((width, band), F32),
                 pltpu.VMEM((width, band), F32),
-                pltpu.VMEM((CHUNKS, part, band), F32),
-                pltpu.VMEM((CHUNKS, part, band), F32),
-                pltpu.VMEM((CHUNKS, part, band), F32),
-                pltpu.VMEM((CHUNKS, part, band), F32),
+                pltpu.VMEM((CHUNKS, 2, part, band // 2), F32),
+                pltpu.VMEM((CHUNKS, 2, part, band // 2), F32),
+                pltpu.VMEM((CHUNKS, 2, part, band // 2), F32),
+                pltpu.VMEM((CHUNKS, 2, part, band // 2), F32),
                 dma((3,)),
                 dma((chips, 3)),
                 dma((chips, 3)),
                 dma((chips, 3)),
                 dma((chips, 3)),
-                dma((CHUNKS,)),
-                dma((CHUNKS,)),
-                dma((CHUNKS,)),
-                dma((CHUNKS,)),
+                dma((CHUNKS, 2)),
+                dma((CHUNKS, 2)),
+                dma((CHUNKS, 2)),
+                dma((CHUNKS, 2)),
                 dma,
                 dma,
-                dma((CHUNKS,)),
+                dma((CHUNKS, 2)),
             ],
             compiler_params=pltpu.CompilerParams(
                 collective_id=0, has_side_effects=True, vmem_limit_bytes=56 * 1024 * 1024

time: 56.1 us -> 58.5 us (1.043)
  Pallas kernels: 54.2 us -> 56.7 us
    pallas_call x1, Pallas kernels: 54.2 us -> 56.7 us  [local(): pl.pallas_call(functools.partial(kernel, rows, cols), out_shape=jax.Shape...]
where the time goes in v6:
time: 58.5 us; the launch traced here: 58.4 us
  Pallas kernels  56.7 us (97%)
  local copies, waits for them, and re-layouts  1.67 us (3%)
    pallas_call x1, Pallas kernels, local(): pl.pallas_call(functools.partial(kernel, rows, cols), out_shape=jax.Shape...  56.7 us
    unnamed x1, local copies, waits for them, and re-layouts  1.67 us

profile of v6, /device:TPU:6, one launch (start us, length us, event | category | flops | bytes accessed | tf_op | source)
XLA Modules:
  0.0 58.4 jit_solution(5411972176018278137)
XLA Ops:
  0.0 56.7 %shard_map.37 = f32[512,128]{1,0:T(8,128)} custom-call(f32[512,128]{1,0:T(8,128)} %x_ref.1, f32[1,256,512]{2,1,0:T(8,128)} %v_ref.1, f32[1,128,512]{2,1,0:T(8,128)} %f_ref.1), custom_call_target="tpu_custom_call" | custom-call | tf_op jit(solution)/shard_map/pallas_call | solution.py:402
  56.7 1.7 %copy.5 = f32[512,128]{1,0:T(8,128)} copy(f32[512,128]{1,0:T(8,128)} %shard_map.37) | data formatting | bytes 524288

commit v7 on v5

--- a/solution.py
+++ b/solution.py
@@ -293,9 +293,14 @@
         zout[i] = at[rows_of(i), :] + product(zin[i], ch[...], cl[...], 0)
         down(i).start()
 
-    def give_back(i):
-        osend[i] = zin[i] + et[rows_of(i), :] + product(zin[i], dh[...], dl[...], 0)
-        back(i).start()
+    def give_back(start, stop):
+        z = zin[start:stop].reshape((stop - start) * part, band)
+        span = pl.ds(start * part, (stop - start) * part)
+        osend[start:stop] = (z + et[span, :] + product(z, dh[...], dl[...], 0)).reshape(stop - start, part, band)
+        for i in range(start, stop):
+            back(i).start()
+
+    middle, late = CHUNKS // 2, 3 * CHUNKS // 4
 
     @pl.when(row < rows // 2)
     def _():
@@ -310,22 +315,23 @@
         def _():
             chain_d()
 
-        for i in range(CHUNKS):
-            give_back(i)
+        give_back(0, middle)
+        give_back(middle, CHUNKS)
 
     @pl.when(row == 1)
     def _():
-        for i in range(CHUNKS):
-            hop(i)
-            give_back(i)
+        for start, stop in ((0, middle), (middle, late), (late, CHUNKS)):
+            for i in range(start, stop):
+                hop(i)
+            give_back(start, stop)
 
     @pl.when(first)
     def _():
         for i in range(CHUNKS):
             down(i).wait_recv()
-            give_back(i)
-            at[rows_of(i), :] = at[rows_of(i), :] + product(zin[i], ch[...], cl[...], 0)
-        out_ref[...] = at[...].T
+            give_back(i, i + 1)
+        z = zin[...].reshape(width, band)
+        out_ref[...] = (at[...] + product(z, ch[...], cl[...], 0)).T
 
     @pl.when(row > 0)
     def _():

time: 56.1 us -> 55.4 us (0.988)
  Pallas kernels: 54.2 us -> 53.6 us
    pallas_call x1, Pallas kernels: 54.2 us -> 53.6 us  [local(): pl.pallas_call(functools.partial(kernel, rows, cols), out_shape=jax.Shape...]
where the time goes in v7:
time: 55.4 us; the launch traced here: 55.2 us
  Pallas kernels  53.6 us (97%)
  local copies, waits for them, and re-layouts  1.67 us (3%)
    pallas_call x1, Pallas kernels, local(): pl.pallas_call(functools.partial(kernel, rows, cols), out_shape=jax.Shape...  53.6 us
    unnamed x1, local copies, waits for them, and re-layouts  1.67 us

profile of v7, /device:TPU:6, one launch (start us, length us, event | category | flops | bytes accessed | tf_op | source)
XLA Modules:
  0.0 55.2 jit_solution(8821795716118222992)
XLA Ops:
  0.0 53.6 %shard_map.37 = f32[512,128]{1,0:T(8,128)} custom-call(f32[512,128]{1,0:T(8,128)} %x_ref.1, f32[1,256,512]{2,1,0:T(8,128)} %v_ref.1, f32[1,128,512]{2,1,0:T(8,128)} %f_ref.1), custom_call_target="tpu_custom_call" | custom-call | tf_op jit(solution)/shard_map/pallas_call | solution.py:376
  53.6 1.7 %copy.5 = f32[512,128]{1,0:T(8,128)} copy(f32[512,128]{1,0:T(8,128)} %shard_map.37) | data formatting | bytes 524288

commit v8 on v7

--- a/solution.py
+++ b/solution.py
@@ -124,13 +124,19 @@
         src_ref=x_ref, dst_ref=xm, send_sem=x_send, recv_sem=x_recv,
         device_id={"col": mate}, device_id_type=MESH)
 
-    for piece in range(3):
+    lends_x = jnp.logical_and(last, jnp.logical_not(holds_upper))
+    for d in range(1, chips):
+        across(d, 0).start()
+
+    @pl.when(lends_x)
+    def _():
+        move_x.start()
+
+    @pl.when(jnp.logical_not(last))
+    def _():
         for d in range(1, chips):
-            across(d, piece).start()
-        if piece == 0:
-            @pl.when(jnp.logical_and(last, jnp.logical_not(holds_upper)))
-            def _():
-                move_x.start()
+            across(d, 1).start()
+
     for piece in (1, 2, 0):
         onward(0, piece).start()
 
@@ -191,6 +197,21 @@
     @pl.when(holds_upper)
     def _():
         make_xu(xt[...])
+
+    for d in range(1, chips):
+        across(d, 0).wait_send()
+
+    @pl.when(lends_x)
+    def _():
+        move_x.wait_send()
+
+    @pl.when(last)
+    def _():
+        for d in range(1, chips):
+            across(d, 1).start()
+
+    for d in range(1, chips):
+        across(d, 2).start()
 
     for d in range(1, chips):
         across(d, 0).wait_recv()
@@ -349,9 +370,6 @@
         for i in range(CHUNKS):
             down_mate(i).wait_send()
 
-    @pl.when(jnp.logical_and(last, jnp.logical_not(holds_upper)))
-    def _():
-        move_x.wait_send()
 
     @pl.when(jnp.logical_not(last))
     def _():
@@ -360,7 +378,7 @@
 
     for piece in range(3):
         for d in range(chips):
-            if d > 0:
+            if d > 0 and piece > 0:
                 across(d, piece).wait_send()
             onward(d, piece).wait_send()
 

time: 55.4 us -> 55.6 us (level)
  no operation moved by 1% of the time
where the time goes in v8:
time: 55.6 us; the launch traced here: 55.5 us
  Pallas kernels  53.8 us (97%)
  local copies, waits for them, and re-layouts  1.67 us (3%)
    pallas_call x1, Pallas kernels, local(): pl.pallas_call(functools.partial(kernel, rows, cols), out_shape=jax.Shape...  53.8 us
    unnamed x1, local copies, waits for them, and re-layouts  1.67 us

profile of v8, /device:TPU:6, one launch (start us, length us, event | category | flops | bytes accessed | tf_op | source)
XLA Modules:
  0.0 55.5 jit_solution(4260921784756139343)
XLA Ops:
  0.0 53.8 %shard_map.37 = f32[512,128]{1,0:T(8,128)} custom-call(f32[512,128]{1,0:T(8,128)} %x_ref.1, f32[1,256,512]{2,1,0:T(8,128)} %v_ref.1, f32[1,128,512]{2,1,0:T(8,128)} %f_ref.1), custom_call_target="tpu_custom_call" | custom-call | tf_op jit(solution)/shard_map/pallas_call | solution.py:394
  53.8 1.7 %copy.5 = f32[512,128]{1,0:T(8,128)} copy(f32[512,128]{1,0:T(8,128)} %shard_map.37) | data formatting | bytes 524288

commit v9 on v7

--- a/solution.py
+++ b/solution.py
@@ -8,7 +8,7 @@
 from jax.sharding import PartitionSpec as P
 
 MESH = pl.DeviceIdType.MESH
-CHUNKS = 8
+CHUNKS = 4
 F32, BF16 = jnp.float32, jnp.bfloat16
 
 

time: 55.4 us -> 59.5 us (1.074)
  Pallas kernels: 53.6 us -> 57.7 us
    pallas_call x1, Pallas kernels: 53.6 us -> 57.7 us  [local(): pl.pallas_call(functools.partial(kernel, rows, cols), out_shape=jax.Shape...]
where the time goes in v9:
time: 59.5 us; the launch traced here: 59.4 us
  Pallas kernels  57.7 us (97%)
  local copies, waits for them, and re-layouts  1.67 us (3%)
    pallas_call x1, Pallas kernels, local(): pl.pallas_call(functools.partial(kernel, rows, cols), out_shape=jax.Shape...  57.7 us
    unnamed x1, local copies, waits for them, and re-layouts  1.67 us

profile of v9, /device:TPU:6, one launch (start us, length us, event | category | flops | bytes accessed | tf_op | source)
XLA Modules:
  0.0 59.4 jit_solution(12026185686828108774)
XLA Ops:
  0.0 57.7 %shard_map.37 = f32[512,128]{1,0:T(8,128)} custom-call(f32[512,128]{1,0:T(8,128)} %x_ref.1, f32[1,256,512]{2,1,0:T(8,128)} %v_ref.1, f32[1,128,512]{2,1,0:T(8,128)} %f_ref.1), custom_call_target="tpu_custom_call" | custom-call | tf_op jit(solution)/shard_map/pallas_call | solution.py:376
  57.7 1.7 %copy.5 = f32[512,128]{1,0:T(8,128)} copy(f32[512,128]{1,0:T(8,128)} %shard_map.37) | data formatting | bytes 524288
